TPU v7x, 32 devices: a whole 2x2x4 slice. The times are simulated.
32 devices in a mesh: tm: 4 (over z), space: 8 (over y, x, core).
Axes of the slice: x: 2, y: 2, z: 4, core: 2. Of those that a mesh axis runs over, the one named last changes fastest.
Arguments:
- snaps: bfloat16 [4096, 3, 16384], P('tm', None, 'space')
- phase_bin: int32 [4096], P('tm'), may hold values from 0 to 15, as said below
- owner_order: int32 [16], replicated, may hold values from 0 to 15, each once
- modes: bfloat16 [16, 128, 3, 16384], P(None, None, None, 'space'), may hold values from -0.02734375 to 0.02734375
Outputs:
- phase_mean: bfloat16 [16, 3, 16384], P('tm', None, 'space')
- coefficients: float32 [4096, 128], P('tm')
Inputs may be any that keep to these rules, and one draw needn't show every extreme that they name: `phase_bin`: every bin is named by at least one snapshot; in each aligned block of 1024 snapshots no bin is named more than 128 times.
All inputs are finite; a program needn't handle non-finite values.
Results may differ from a plain program's by a relative error of at most 0.0068.
Values may be sent and summed in bfloat16 or wider, within the bound.
A program may use at most 192 MiB of HBM per device.

v0:
```python
import jax
import jax.numpy as jnp
from jax import lax
from jax.sharding import PartitionSpec as P


def on_device(snaps, phase_bin, owner_order, modes):
    snap_rows = snaps.shape[0]
    cell_count = snaps.shape[2]
    bin_total = modes.shape[0]
    mode_count = modes.shape[1]
    width = 3 * cell_count
    capacity = 2 * snap_rows // bin_total
    flattened = snaps.reshape(snap_rows, width)
    bin_ids = lax.broadcasted_iota(jnp.int32, (bin_total, 1), 0)
    matches = phase_bin[None, :] == bin_ids
    onehot = matches.astype(jnp.bfloat16)
    reorder = (owner_order[:, None] == bin_ids[:, 0][None, :]).astype(jnp.bfloat16)
    chosen = jnp.dot(reorder, onehot, preferred_element_type=jnp.float32)
    chosen_bf = chosen.astype(jnp.bfloat16)
    partial_sums = jnp.dot(chosen_bf, flattened, preferred_element_type=jnp.float32)
    partial_counts = jnp.sum(chosen, axis=1)
    total_sums, total_counts = lax.psum((partial_sums, partial_counts), "tm")
    all_mean = (total_sums / total_counts[:, None]).astype(jnp.bfloat16)
    own_rows = bin_total // lax.axis_size("tm")
    own_mean = lax.dynamic_slice_in_dim(all_mean, lax.axis_index("tm") * own_rows, own_rows, 0)
    phase_mean = own_mean.reshape(own_mean.shape[0], 3, cell_count)
    row_numbers = jnp.arange(bin_total, dtype=jnp.int32)
    inverse = jnp.zeros((bin_total,), jnp.int32).at[owner_order].set(row_numbers)
    mean_by_bin = jnp.take(all_mean, inverse, axis=0)
    match_int = matches.astype(jnp.int32)
    ranks = jnp.cumsum(match_int, axis=1) - 1
    slot = jnp.sum(match_int * ranks, axis=0)
    target = phase_bin * capacity + slot
    snap_numbers = jnp.arange(snap_rows, dtype=jnp.int32)
    source = jnp.full((bin_total * capacity,), snap_rows, jnp.int32).at[target].set(snap_numbers)
    gathered = jnp.take(flattened, source, axis=0, mode="fill", fill_value=0)
    gathered = gathered.reshape(bin_total, capacity, width)
    grouped = (gathered.astype(jnp.float32) - mean_by_bin.astype(jnp.float32)[:, None, :]).astype(
        jnp.bfloat16
    )
    modes_flat = modes.reshape(bin_total, mode_count, width)
    products = lax.dot_general(
        grouped, modes_flat, (((2,), (2,)), ((0,), (0,))), preferred_element_type=jnp.float32
    )
    picked = jnp.take(products.reshape(bin_total * capacity, mode_count), target, axis=0)
    coefficients = lax.psum(picked, "space")
    return (phase_mean, coefficients)


def solution(mesh):
    in_specs = (P("tm", None, "space"), P("tm"), P(), P(None, None, None, "space"))
    out_specs = (P("tm", None, "space"), P("tm", None))
    return jax.shard_map(
        on_device, mesh=mesh, in_specs=in_specs, out_specs=out_specs, check_vma=False
    )
```

profile of v0, /device:TPU:0, one launch (start us, length us, event | category | flops | bytes accessed | tf_op | source)
XLA Modules:
  0.0 239.0 jit_solution(14934051923834580583)
XLA Ops:
  7.2 0.0 copy-start
  7.2 0.0 copy-start.1
  7.2 0.0 all-reduce.3.cloned.1.call-start
  7.2 16.7 %copy.9 = bf16[1024,3,2048]{0,2,1:T(8,128)(2,1)} copy(bf16[1024,3,2048]{2,0,1:T(8,128)(2,1)} %param.4) | data formatting | bytes 25165824 | tf_op args[0]
  23.9 0.0 copy-done
  23.9 0.0 copy-done.1
  23.9 0.3 fusion.17
  24.2 8.7 %fusion.7 = f32[16,6144]{1,0:T(8,128)} fusion(bf16[1024,6144]{0,1:T(8,128)(2,1)} %bitcast.19, bf16[16,1024]{1,0:T(8,128)(2,1)S(1)} %get-tuple-element.5), kind=kOutput, calls=%fused_computation.19 | convolution fusion | flops 201326592 | bytes 13008896 | tf_op jit(solution)/shard_map/dot_general | solution.py:21
  32.9 0.0 all-reduce.3.cloned.1.call-update
  32.9 0.0 all-reduce.5.cloned.1.call-start
  33.0 16.7 %copy.12 = bf16[1024,6144]{1,0:T(8,128)(2,1)} copy(bf16[1024,6144]{0,1:T(8,128)(2,1)} %bitcast.20) | data formatting | bytes 25165824 | tf_op jit(solution)/shard_map/reshape | solution.py:14
  49.7 0.6 scatter_custom_fusion.1
  50.3 13.5 %psum.22 = f32[16]{0:T(128)S(1)} all-reduce(f32[16]{0:T(128)S(1)} %get-tuple-element.4), channel_id=1, replica_groups=mesh['tm'=4,'space'=8] {'tm'}, use_global_device_ids=true, to_apply=%region_2.0 | all-reduce | flops 16 | bytes 128 | tf_op jit(solution)/shard_map/psum | solution.py:23
  63.8 4.5 %reduce-window.6 = s32[16,8,128]{2,1,0:T(8,128)S(1)} reduce-window(s32[16,8,128]{2,1,0:T(8,128)S(1)} %fusion.5, s32[]{:T(128)} %constant.40.clone.1), window={size=1x1x128 pad=0_0x0_0x127_0}, to_apply=%region_3.0 | reduce-window | flops 2080768 | bytes 131076 | tf_op jit(solution)/shard_map/reduce-window
  68.4 0.1 slice.14
  68.4 0.1 copy.10
  68.6 0.1 copy.11
  68.7 0.1 select_reduce_fusion
  68.8 4.5 %scatter_custom_fusion = s32[2048]{0:T(1024)S(1)} fusion(s32[1024]{0:T(1024)S(1)} %get-tuple-element.3, s32[1024]{0:T(1024)S(1)} %iota.22, s32[]{:T(128)} %constant.65.clone.1), kind=kCustom, calls=%fused_computation.29 | custom fusion | bytes 8196 | tf_op jit(solution)/shard_map/scatter | solution.py:36
  73.3 32.6 %copy.13 = bf16[16,128,3,2048]{1,3,2,0:T(8,128)(2,1)} copy(bf16[16,128,3,2048]{3,1,2,0:T(8,128)(2,1)} %param.7) | data formatting | bytes 50331648 | tf_op args[3]
  106.0 48.0 %gather_fusion = bf16[2048,6144]{1,0:T(8,128)(2,1)} fusion(bf16[1024,6144]{1,0:T(8,128)(2,1)} %copy.12, s32[2048]{0:T(1024)S(1)} %fusion.10), kind=kCustom, calls=%fused_computation | custom fusion | bytes 50339840 | tf_op jit(solution)/shard_map/jit(_take)/gather | solution.py:37
  154.0 0.0 all-reduce.3.cloned.1.call-done
  154.0 1.1 divide_convert_fusion
  155.1 0.7 gather_fusion.1
  155.8 0.1 select_convert_fusion
  155.9 17.7 %fusion = f32[16,128,128]{2,1,0:T(8,128)S(1)} fusion(bf16[16,128,6144]{1,2,0:T(8,128)(2,1)} %bitcast.21, f32[16,6144]{1,0:T(8,128)S(1)} %select_convert_fusion, bf16[16,128,6144]{2,1,0:T(8,128)(2,1)} %bitcast.22, pred[16,128]{1,0:T(8,128)(4,1)S(1)} %and_bitcast_fusion), kind=kOutput, calls=%fused_computation.6 | convolution fusion | flops 3271557120 | bytes 51775488 | tf_op jit(solution)/shard_map/dot_general | solution.py:43
  173.6 2.8 %gather_fusion.2 = f32[1024,128]{1,0:T(8,128)S(1)} fusion(f32[2048,128]{1,0:T(8,128)S(1)} %bitcast.23, s32[1024]{0:T(1024)S(1)} %broadcast_clamp_fusion), kind=kCustom, calls=%fused_computation.2 | custom fusion | bytes 1052672 | tf_op jit(solution)/shard_map/jit(_take)/gather | solution.py:46
  176.4 1.0 broadcast_select_fusion
  177.4 0.0 all-reduce.5.cloned.1.call-update
  177.4 0.7 constant_dynamic-slice_fusion
  178.1 52.2 %all-reduce.5.cloned.1.call-done = f32[1024,128]{1,0:T(8,128)} async-done(((f32[1024,128]{1,0:T(8,128)}), f32[1024,128]{1,0:T(8,128)}) %all-reduce.5.cloned.1.call-update) | async-done | bytes 524304 | tf_op jit(solution)/shard_map/psum | solution.py:47
  230.3 1.9 copy.18
  (13 shorter events, 0.1 us)
Async XLA Ops:
  7.2 16.8 %copy-start = (s32[1024]{0:T(1024)S(1)}, s32[1024]{0:T(1024)}, u32[]{:S(2)}) copy-start(s32[1024]{0:T(1024)} %param.5) | copy-start | bytes 12292
  7.2 16.7 %copy-start.1 = (s32[16]{0:T(128)S(1)}, s32[16]{0:T(128)}, u32[]{:S(2)}) copy-start(s32[16]{0:T(128)} %param.6) | copy-start | bytes 196
  7.2 146.8 %all-reduce.3.cloned.1.call-start = ((), (), s32[]{:S(2)}) async-start(), calls=%async_computation | async-start | bytes 786432 | tf_op jit(solution)/shard_map/psum | solution.py:23
  32.9 197.3 %all-reduce.5.cloned.1.call-start = ((), (), s32[]{:S(2)}) async-start(), calls=%async_computation.1 | async-start | bytes 1048576 | tf_op jit(solution)/shard_map/psum | solution.py:47
Sparse Core Ops, SparseCore 0:
  33.1 39.8 all-reduce.2
  177.5 52.6 all-reduce.4
where the time goes:
time: 241 us; the launch traced here: 239 us
  local copies, waits for them, and re-layouts  125 us (52%)
  waiting for transfers between devices  52.2 us (22%)
  matrix products  26.7 us (11%)
  between operations  14.2 us (6%)
  blocking collectives  13.5 us (6%)
  other arithmetic  6.89 us (3%)
    psum x1, waiting for transfers between devices, on_device(): coefficients = lax.psum(picked, 'space')  52.2 us
    unnamed x7, local copies, waits for them, and re-layouts  51.2 us
    gather x1, local copies, waits for them, and re-layouts, on_device(): gathered = jnp.take(flattened, source, axis=0, mode='fill', fill_value=0)  48 us
    dot_general x1, matrix products, on_device(): lax.dot_general(grouped, modes_flat, (((2,), (2,)), ((0,), (0,))), prefer...  17.7 us
    reshape x1, local copies, waits for them, and re-layouts, on_device(): flattened = snaps.reshape(snap_rows, width)  16.7 us
    psum x1, blocking collectives, on_device(): total_sums, total_counts = lax.psum((partial_sums, partial_counts), 'tm')  13.5 us
    dot_general x1, matrix products, on_device(): jnp.dot(chosen_bf, flattened, preferred_element_type=jnp.float32)  8.7 us
  transfers between devices with their start and end apart: 2, of which 1 were waited for; matrix products, arithmetic and copies ran while one was open for 45% of the time, Pallas kernels for 0%

commit v1 on v0

--- a/solution.py
+++ b/solution.py
@@ -44,7 +44,8 @@
         grouped, modes_flat, (((2,), (2,)), ((0,), (0,))), preferred_element_type=jnp.float32
     )
     picked = jnp.take(products.reshape(bin_total * capacity, mode_count), target, axis=0)
-    coefficients = lax.psum(picked, "space")
+    pieces = lax.all_gather(picked, "space")
+    coefficients = jnp.sum(pieces, axis=0)
     return (phase_mean, coefficients)
 
 

time: 241 us -> 224 us (0.929)
  waiting for transfers between devices: 52.2 us -> 34.5 us
  other arithmetic: 6.89 us -> 10.1 us
    psum x1 -> x0, waiting for transfers between devices: 52.2 us -> none  [on_device(): coefficients = lax.psum(picked, 'space')]
    all_gather x0 -> x1, waiting for transfers between devices: none -> 34.4 us  [on_device(): pieces = lax.all_gather(picked, 'space')]
    reduce_sum x0 -> x1, other arithmetic: none -> 3.24 us  [on_device(): coefficients = jnp.sum(pieces, axis=0)]
    unnamed x7 -> x6, local copies, waits for them, and re-layouts: 51.2 us -> 49.3 us
  transfers between devices with their start and end apart: 2 -> 2, of which waited for: 1 -> 1; matrix products, arithmetic and copies ran while one was open for 45% -> 49% of each run, Pallas kernels for 0% -> 0%
where the time goes in v1:
time: 224 us; the launch traced here: 223 us
  local copies, waits for them, and re-layouts  124 us (55%)
  waiting for transfers between devices  34.5 us (15%)
  matrix products  26.7 us (12%)
  between operations  14.2 us (6%)
  blocking collectives  13.5 us (6%)
  other arithmetic  10.1 us (5%)
    unnamed x6, local copies, waits for them, and re-layouts  49.3 us
    gather x1, local copies, waits for them, and re-layouts, on_device(): gathered = jnp.take(flattened, source, axis=0, mode='fill', fill_value=0)  48 us
    all_gather x1, waiting for transfers between devices, on_device(): pieces = lax.all_gather(picked, 'space')  34.4 us
    dot_general x1, matrix products, on_device(): lax.dot_general(grouped, modes_flat, (((2,), (2,)), ((0,), (0,))), prefer...  17.7 us
    reshape x1, local copies, waits for them, and re-layouts, on_device(): flattened = snaps.reshape(snap_rows, width)  16.7 us
    psum x1, blocking collectives, on_device(): total_sums, total_counts = lax.psum((partial_sums, partial_counts), 'tm')  13.5 us
    dot_general x1, matrix products, on_device(): jnp.dot(chosen_bf, flattened, preferred_element_type=jnp.float32)  8.7 us
    another operation x2, other arithmetic  4.55 us
  transfers between devices with their start and end apart: 2, of which 1 were waited for; matrix products, arithmetic and copies ran while one was open for 49% of the time, Pallas kernels for 0%

profile of v1, /device:TPU:0, one launch (start us, length us, event | category | flops | bytes accessed | tf_op | source)
XLA Modules:
  0.0 222.5 jit_solution(3637983912926417796)
XLA Ops:
  7.2 0.0 copy-start
  7.2 0.0 copy-start.1
  7.2 0.0 all-reduce.2.cloned.1.call-start
  7.2 16.7 %copy.15 = bf16[1024,3,2048]{0,2,1:T(8,128)(2,1)} copy(bf16[1024,3,2048]{2,0,1:T(8,128)(2,1)} %param.4) | data formatting | bytes 25165824 | tf_op args[0]
  23.9 0.0 copy-done
  23.9 0.0 copy-done.1
  23.9 0.3 fusion.17
  24.2 8.7 %fusion.7 = f32[16,6144]{1,0:T(8,128)} fusion(bf16[1024,6144]{0,1:T(8,128)(2,1)} %bitcast.21, bf16[16,1024]{1,0:T(8,128)(2,1)S(1)} %get-tuple-element.5), kind=kOutput, calls=%fused_computation.19 | convolution fusion | flops 201326592 | bytes 13008896 | tf_op jit(solution)/shard_map/dot_general | solution.py:21
  32.9 0.0 all-reduce.2.cloned.1.call-update
  32.9 0.0 all-gather.2.cloned.1.call-start
  33.0 16.7 %copy.18 = bf16[1024,6144]{1,0:T(8,128)(2,1)} copy(bf16[1024,6144]{0,1:T(8,128)(2,1)} %bitcast.22) | data formatting | bytes 25165824 | tf_op jit(solution)/shard_map/reshape | solution.py:14
  49.7 0.6 scatter_custom_fusion.1
  50.3 13.5 %psum.15 = f32[16]{0:T(128)S(1)} all-reduce(f32[16]{0:T(128)S(1)} %get-tuple-element.4), channel_id=1, replica_groups=mesh['tm'=4,'space'=8] {'tm'}, use_global_device_ids=true, to_apply=%region_2.0 | all-reduce | flops 16 | bytes 128 | tf_op jit(solution)/shard_map/psum | solution.py:23
  63.8 4.5 %reduce-window.6 = s32[16,8,128]{2,1,0:T(8,128)S(1)} reduce-window(s32[16,8,128]{2,1,0:T(8,128)S(1)} %fusion.5, s32[]{:T(128)} %constant.40.clone.1), window={size=1x1x128 pad=0_0x0_0x127_0}, to_apply=%region_3.0 | reduce-window | flops 2080768 | bytes 131076 | tf_op jit(solution)/shard_map/reduce-window
  68.4 0.1 slice.14
  68.4 0.1 copy.16
  68.6 0.1 copy.17
  68.7 0.1 select_reduce_fusion
  68.8 4.5 %scatter_custom_fusion = s32[2048]{0:T(1024)S(1)} fusion(s32[1024]{0:T(1024)S(1)} %get-tuple-element.3, s32[1024]{0:T(1024)S(1)} %iota.22, s32[]{:T(128)} %constant.65.clone.1), kind=kCustom, calls=%fused_computation.29 | custom fusion | bytes 8196 | tf_op jit(solution)/shard_map/scatter | solution.py:36
  73.3 32.6 %copy.19 = bf16[16,128,3,2048]{1,3,2,0:T(8,128)(2,1)} copy(bf16[16,128,3,2048]{3,1,2,0:T(8,128)(2,1)} %param.7) | data formatting | bytes 50331648 | tf_op args[3]
  105.9 48.0 %gather_fusion = bf16[2048,6144]{1,0:T(8,128)(2,1)} fusion(bf16[1024,6144]{1,0:T(8,128)(2,1)} %copy.18, s32[2048]{0:T(1024)S(1)} %fusion.10), kind=kCustom, calls=%fused_computation | custom fusion | bytes 50339840 | tf_op jit(solution)/shard_map/jit(_take)/gather | solution.py:37
  154.0 0.0 all-reduce.2.cloned.1.call-done
  154.0 1.1 divide_convert_fusion
  155.1 0.7 gather_fusion.1
  155.8 0.1 select_convert_fusion
  155.9 17.7 %fusion = f32[16,128,128]{2,1,0:T(8,128)S(1)} fusion(bf16[16,128,6144]{1,2,0:T(8,128)(2,1)} %bitcast.23, f32[16,6144]{1,0:T(8,128)S(1)} %select_convert_fusion, bf16[16,128,6144]{2,1,0:T(8,128)(2,1)} %bitcast.24, pred[16,128]{1,0:T(8,128)(4,1)S(1)} %and_bitcast_fusion), kind=kOutput, calls=%fused_computation.6 | convolution fusion | flops 3271557120 | bytes 51775488 | tf_op jit(solution)/shard_map/dot_general | solution.py:43
  173.6 2.8 %gather_fusion.2 = f32[1024,128]{1,0:T(8,128)S(1)} fusion(f32[2048,128]{1,0:T(8,128)S(1)} %bitcast.25, s32[1024]{0:T(1024)S(1)} %broadcast_clamp_fusion), kind=kCustom, calls=%fused_computation.2 | custom fusion | bytes 1052672 | tf_op jit(solution)/shard_map/jit(_take)/gather | solution.py:46
  176.4 1.0 bitcast_select_fusion
  177.4 0.0 all-gather.2.cloned.1.call-update
  177.4 0.7 constant_dynamic-slice_fusion
  178.1 34.4 %all-gather.2.cloned.1.call-done = f32[8,1024,128]{2,1,0:T(8,128)} async-done(((f32[1,1024,128]{2,1,0:T(8,128)}), f32[8,1024,128]{2,1,0:T(8,128)}) %all-gather.2.cloned.1.call-update) | async-done | bytes 4194320 | tf_op jit(solution)/shard_map/all_gather | solution.py:47
  212.5 3.2 %reduce_sum.32 = f32[1024,128]{1,0:T(8,128)} reduce(f32[8,1024,128]{2,1,0:T(8,128)} %all-gather.2.cloned.1.call-done, f32[]{:T(128)} %constant.31.clone.1), dimensions={0}, to_apply=%region_8.9 | reduce | flops 917504 | bytes 4718596 | tf_op jit(solution)/shard_map/reduce_sum | solution.py:48
  (13 shorter events, 0.1 us)
Async XLA Ops:
  7.2 16.8 %copy-start = (s32[1024]{0:T(1024)S(1)}, s32[1024]{0:T(1024)}, u32[]{:S(2)}) copy-start(s32[1024]{0:T(1024)} %param.5) | copy-start | bytes 12292
  7.2 16.7 %copy-start.1 = (s32[16]{0:T(128)S(1)}, s32[16]{0:T(128)}, u32[]{:S(2)}) copy-start(s32[16]{0:T(128)} %param.6) | copy-start | bytes 196
  7.2 146.8 %all-reduce.2.cloned.1.call-start = ((), (), s32[]{:S(2)}) async-start(), calls=%async_computation | async-start | bytes 786432 | tf_op jit(solution)/shard_map/psum | solution.py:23
  32.9 179.5 %all-gather.2.cloned.1.call-start = ((), (), s32[]{:S(2)}) async-start(), calls=%async_computation.1 | async-start | bytes 4718592 | tf_op jit(solution)/shard_map/all_gather | solution.py:47
Sparse Core Ops, SparseCore 0:
  33.1 39.8 all-reduce.1
  177.5 34.8 all-gather.1
